TPU v7x, 32 devices: a whole 2x2x4 slice. The times are simulated.
32 devices in a mesh: dp: 4 (over y, x), region: 8 (over z, core).
Axes of the slice: x: 2, y: 2, z: 4, core: 2. Of those that a mesh axis runs over, the one named last changes fastest.
Arguments:
- leaves: float32 [128, 64, 1024], P('region', None, 'dp'), may hold values from -280 to 0
- weights: float32 [2, 128, 8, 64, 64], P(None, 'region'), may hold values from 0.00048828125 to 0.0078125
- groups: int32 [2, 8, 8, 2], P(None, None, 'region'), may hold values from 0 to 15
- prod_kids: int32 [2, 256, 2], P(None, 'region'), may hold values from 0 to 15
- sum_kids: int32 [2, 128, 8], P(None, 'region'), may hold values from 0 to 31
- cotangent: float32 [128, 64, 1024], P('region', None, 'dp'), may hold values from -6 to 6
Outputs:
- top_logp: float32 [128, 64, 1024], P('region', None, 'dp')
- leaf_grad: float32 [128, 64, 1024], P('region', None, 'dp')
- weight_flow: float32 [2, 128, 8, 64, 64], P(None, 'region')
All inputs are finite; a program needn't handle non-finite values.
Results may differ from a plain program's by a relative error of at most 0.0003.
Values sent between devices are 32-bit elements; how exact they have to be, the bound alone decides.
A program may use at most 128 MiB of HBM per device.

v0:
```python
import jax
import jax.numpy as jnp
from jax import lax
from jax.sharding import PartitionSpec as P


def send_home(slot_gradient, owner_hot):
    return jnp.einsum(
        "rb,rjs->bjs",
        owner_hot,
        lax.all_to_all(slot_gradient, "region", split_axis=0, concat_axis=0, tiled=True),
        precision=lax.Precision.HIGHEST,
    )


def per_device(leaves, weights, groups, prod_kids, sum_kids, cotangent):
    maximum_value = lax.Precision.HIGHEST
    levels = weights.shape[0]
    local_blocks = leaves.shape[0]
    prod_count = prod_kids.shape[1]
    samples_all = leaves.shape[2] * lax.axis_size("dp")
    saved = []
    level_in = leaves
    for level in range(levels):
        slot_ids = groups[level][:, 0, :].reshape(-1)
        outgoing = level_in[slot_ids]
        kid_pairs = prod_kids[level]
        received = lax.all_to_all(outgoing, "region", split_axis=0, concat_axis=0, tiled=True)
        prods = received[kid_pairs[:, 0]] + received[kid_pairs[:, 1]]
        chosen = prods[sum_kids[level]]
        shift_top = jnp.max(chosen, axis=(1, 2), keepdims=True)
        exponent = jnp.exp(chosen - shift_top)
        running_totals = jnp.einsum(
            "bkij,bkjs->bis", weights[level], exponent, precision=maximum_value
        )
        level_in = shift_top[:, 0] + jnp.log(running_totals)
        saved.append((exponent, running_totals, slot_ids))
    grad_out = cotangent
    flow_parts = [None] * levels
    for level in reversed(range(levels)):
        exponent, running_totals, slot_ids = saved[level]
        ratio = grad_out / running_totals
        grad_chosen = (
            jnp.einsum("bkij,bis->bkjs", weights[level], ratio, precision=maximum_value) * exponent
        )
        chooser = (
            sum_kids[level][:, :, None] == jnp.arange(prod_count, dtype=jnp.int32)[None, None, :]
        ).astype(jnp.float32)
        product_gradients = jnp.einsum(
            "bkp,bkjs->pjs", chooser, grad_chosen, precision=maximum_value
        )
        slot_total = groups.shape[1] * groups.shape[3]
        reference_onehot = (
            prod_kids[level][:, :, None] == jnp.arange(slot_total, dtype=jnp.int32)[None, None, :]
        ).astype(jnp.float32)
        slot_gradient = jnp.einsum(
            "hba,hue->aue", reference_onehot, product_gradients, precision=maximum_value
        )
        owner_hot = (
            slot_ids[:, None] == jnp.arange(local_blocks, dtype=jnp.int32)[None, :]
        ).astype(jnp.float32)
        flow_part = jnp.einsum("bis,bkjs->bkij", ratio, exponent, precision=maximum_value)
        grad_next = send_home(slot_gradient, owner_hot)
        flow_part = lax.psum(flow_part, "dp")
        flow_parts[level] = flow_part
        grad_out = grad_next
    weight_flow = jnp.stack(flow_parts, axis=0) / samples_all
    return (level_in, grad_out, weight_flow)


def solution(mesh):
    placed = (
        P("region", None, "dp"),
        P(None, "region", None, None, None),
        P(None, None, "region", None),
        P(None, "region", None),
        P(None, "region", None),
        P("region", None, "dp"),
    )
    return jax.shard_map(
        per_device,
        mesh=mesh,
        in_specs=placed,
        out_specs=(
            P("region", None, "dp"),
            P("region", None, "dp"),
            P(None, "region", None, None, None),
        ),
        check_vma=False,
    )
```

profile of v0, /device:TPU:0, one launch (start us, length us, event | category | flops | bytes accessed | tf_op | source)
XLA Modules:
  0.0 410.0 jit_solution(5266751619671039632)
XLA Ops:
  7.2 0.0 copy-start
  7.2 0.8 fusion.52
  8.0 0.1 copy.56
  8.1 0.1 reshape_squeeze_squeeze.6
  8.1 0.3 copy-done
  8.4 1.6 gather_fusion
  10.0 6.3 %all-to-all-start = ((f32[16,64,256]{2,1,0:T(8,128)}), f32[16,64,256]{2,1,0:T(8,128)S(1)}, u32[]{:S(2)}, u32[]{:S(2)}) async-start(f32[16,64,256]{2,1,0:T(8,128)} %gather_fusion), calls=%async_computation | async-start | bytes 2097152 | tf_op jit(solution)/shard_map/all_to_all | solution.py:28
  16.3 0.7 compare_select_fusion
  17.0 0.1 copy.57
  17.1 0.1 reshape.154
  17.2 0.1 copy.58
  17.3 0.1 reshape_squeeze_squeeze.7
  17.4 0.7 slice_bitcast_fusion.4
  18.1 24.8 %all-to-all-done = f32[16,64,256]{2,1,0:T(8,128)S(1)} async-done(((f32[16,64,256]{2,1,0:T(8,128)}), f32[16,64,256]{2,1,0:T(8,128)S(1)}, u32[]{:S(2)}, u32[]{:S(2)}) %all-to-all-start) | async-done | bytes 1048608 | tf_op jit(solution)/shard_map/all_to_all | solution.py:28
  42.9 2.0 gather_fusion.1
  44.9 2.0 gather_fusion.2
  47.0 2.5 add.85
  49.5 4.5 %gather_fusion.3 = f32[128,64,256]{2,1,0:T(8,128)} fusion(f32[32,64,256]{2,1,0:T(8,128)S(1)} %add.85, s32[1024]{0:T(1024)S(1)} %pad_clamp_fusion.4), kind=kCustom, calls=%fused_computation.3 | custom fusion | bytes 16777728 | tf_op jit(solution)/shard_map/gather | solution.py:30
  54.0 4.8 %reduce.2 = f32[128,256]{1,0:T(8,128)S(1)} reduce(f32[128,64,256]{2,1,0:T(8,128)} %gather_fusion.3, f32[]{:T(128)} %constant.1.clone.1), dimensions={1}, to_apply=%region_0.0 | reduce | flops 2064384 | bytes 8519684 | tf_op jit(solution)/shard_map/reduce_max | solution.py:31
  58.9 13.4 %log_add_fusion.1 = (f32[16,64,256]{2,1,0:T(8,128)S(1)}, f32[16,64,256]{2,1,0:T(8,128)}) fusion(f32[16,256]{1,0:T(8,128)S(1)} %bitcast_reduce_fusion.1, f32[2,16,8,64,64]{4,3,2,1,0:T(8,128)} %param.7, f32[16,8,64,256]{3,2,1,0:T(8,128)} %bitcast.128), kind=kOutput, calls=%fused_computation.43 | convolution fusion | flops 1612972032 | bytes 14712832 | tf_op jit(solution)/shard_map/bkij,bkjs->bis/dot_general | solution.py:33
  72.2 1.6 gather_fusion.4
  73.8 4.1 all-to-all-start.1
  77.9 0.1 copy.59
  78.0 0.1 reshape.186
  78.0 8.4 %slice_bitcast_fusion = (f32[16,8,64,64]{3,2,1,0:T(8,128)}, f32[16,8,64,64]{3,2,1,0:T(8,128)}) fusion(f32[2,16,8,64,64]{4,3,2,1,0:T(8,128)} %param.7), kind=kLoop, calls=%fused_computation.21 | loop fusion | bytes 8388608 | tf_op jit(solution)/shard_map/squeeze | solution.py:34
  86.4 5.4 %copy.64 = f32[16,8,64,64]{2,3,1,0:T(8,128)} copy(f32[16,8,64,64]{3,2,1,0:T(8,128)} %get-tuple-element.17) | data formatting | bytes 4194304 | tf_op jit(solution)/shard_map/squeeze | solution.py:34
  91.8 0.0 copy-done.5
  91.8 0.1 copy.63
  91.9 12.4 %all-to-all-done.1 = f32[16,64,256]{2,1,0:T(8,128)S(1)} async-done(((f32[16,64,256]{2,1,0:T(8,128)}), f32[16,64,256]{2,1,0:T(8,128)S(1)}, u32[]{:S(2)}, u32[]{:S(2)}) %all-to-all-start.1) | async-done | bytes 1048608 | tf_op jit(solution)/shard_map/all_to_all | solution.py:28
  104.4 2.0 gather_fusion.5
  106.4 2.0 gather_fusion.6
  108.4 2.5 add.92
  110.9 4.3 %gather_fusion.7 = f32[128,64,256]{2,1,0:T(8,128)} fusion(f32[32,64,256]{2,1,0:T(8,128)S(1)} %add.92, s32[1024]{0:T(1024)S(1)} %pad_clamp_fusion), kind=kCustom, calls=%fused_computation.7 | custom fusion | bytes 16777728 | tf_op jit(solution)/shard_map/gather | solution.py:30
  115.3 4.8 %reduce.4 = f32[128,256]{1,0:T(8,128)S(1)} reduce(f32[128,64,256]{2,1,0:T(8,128)} %gather_fusion.7, f32[]{:T(128)} %constant.1.clone.1), dimensions={1}, to_apply=%region_1.0 | reduce | flops 2064384 | bytes 8519684 | tf_op jit(solution)/shard_map/reduce_max | solution.py:31
  120.1 0.0 copy-start.4
  120.2 13.4 %log_add_fusion = (f32[16,64,256]{2,1,0:T(8,128)}, f32[16,64,256]{2,1,0:T(8,128)S(1)}) fusion(f32[16,256]{1,0:T(8,128)S(1)} %bitcast_reduce_fusion, f32[2,16,8,64,64]{4,3,2,1,0:T(8,128)} %param.7, f32[16,8,64,256]{3,2,1,0:T(8,128)} %bitcast.131), kind=kOutput, calls=%fused_computation.42 | convolution fusion | flops 1612972032 | bytes 14712832 | tf_op jit(solution)/shard_map/bkij,bkjs->bis/dot_general | solution.py:33
  133.5 9.1 %fusion.49 = f32[16,256,512]{1,2,0} fusion(f32[16,64,512]{1,2,0:T(8,128)S(1)} %bitcast.136, f32[16,64,256]{2,1,0:T(8,128)S(1)} %copy-done.4, f32[16,64,256]{2,1,0:T(8,128)S(1)} %get-tuple-element.34), kind=kOutput, calls=%fused_computation.91 | convolution fusion | flops 1610874880 | bytes 12582912
  142.6 12.0 %fusion.8 = f32[16,8,64,256]{3,2,1,0:T(8,128)} fusion(f32[16,8,64,256]{3,2,1,0:T(8,128)} %bitcast.135, f32[16,8,64,256]{3,2,1,0:T(8,128)} %bitcast.132, f32[16,256]{1,0:T(8,128)S(1)} %bitcast_reduce_fusion), kind=kLoop, calls=%fused_computation.19 | loop fusion | flops 4194304 | bytes 25182208 | tf_op jit(solution)/shard_map/mul | solution.py:44
  154.6 10.9 %fusion.2 = f32[32,64,256,1]{2,0,3,1:T(8,128)S(1)} fusion(f32[16,8,64,256]{3,2,1,0:T(8,128)} %fusion.8, s32[16,8]{1,0:T(8,128)S(1)} %copy.63), kind=kOutput, calls=%fused_computation.11 | convolution fusion | flops 805310464 | bytes 10486272 | tf_op jit(solution)/shard_map/bkp,bkjs->pjs/dot_general | solution.py:49
  165.5 1.1 fusion.18
  166.6 1.6 copy.66
  168.2 4.5 %all-to-all-start.2 = ((f32[16,64,256]{2,1,0:T(8,128)}), f32[16,64,256]{2,1,0:T(8,128)}, u32[]{:S(2)}, u32[]{:S(2)}) async-start(f32[16,64,256]{2,1,0:T(8,128)} %copy.66), calls=%async_computation.2 | async-start | bytes 2097152 | tf_op jit(solution)/shard_map/all_to_all | solution.py:11
  172.7 0.0 all-reduce.3.cloned.1.call-start
  172.7 0.1 eq.97
  172.8 5.4 %copy.69 = f32[16,8,64,64]{2,3,1,0:T(8,128)} copy(f32[16,8,64,64]{3,2,1,0:T(8,128)} %get-tuple-element.18) | data formatting | bytes 4194304 | tf_op jit(solution)/shard_map/squeeze | solution.py:34
  178.2 0.1 copy.61
  178.3 11.7 %fusion.14 = f32[1,16,8,64,64]{3,4,2,1,0:T(8,128)} fusion(f32[16,8,64,256]{3,2,1,0:T(8,128)} %bitcast.133, f32[16,256]{1,0:T(8,128)S(1)} %bitcast_reduce_fusion, f32[16,64,256]{2,1,0:T(8,128)S(1)} %copy-done.4, f32[16,64,256]{2,1,0:T(8,128)S(1)} %get-tuple-element.34), kind=kOutput, calls=%fused_computation.27 | convolution fusion | flops 1612972032 | bytes 12599296 | tf_op jit(solution)/shard_map/bis,bkjs->bkij/dot_general | solution.py:62
  189.9 9.3 %all-to-all-done.2 = f32[16,64,256]{2,1,0:T(8,128)} async-done(((f32[16,64,256]{2,1,0:T(8,128)}), f32[16,64,256]{2,1,0:T(8,128)}, u32[]{:S(2)}, u32[]{:S(2)}) %all-to-all-start.2) | async-done | bytes 1048608 | tf_op jit(solution)/shard_map/all_to_all | solution.py:11
  199.3 2.4 fusion.26
  201.7 12.2 %fusion.15 = f32[1,16,8,64,64]{3,4,2,1,0:T(8,128)} fusion(f32[16,8,64,256]{3,2,1,0:T(8,128)} %bitcast.129, f32[16,256]{1,0:T(8,128)S(1)} %bitcast_reduce_fusion.1, f32[16,64,256]{2,1,0:T(8,128)S(1)} %copy-done.3, f32[16,64,256]{2,0,1:T(8,128)S(1)} %fusion.26), kind=kOutput, calls=%fused_computation.28 | convolution fusion | flops 1612972032 | bytes 12599296 | tf_op jit(solution)/shard_map/bis,bkjs->bkij/dot_general | solution.py:62
  213.8 0.0 all-reduce.3.cloned.1.call-update
  213.9 11.2 %fusion.51 = f32[16,256,512]{1,2,0} fusion(f32[16,64,512]{1,2,0:T(8,128)} %bitcast.137, f32[16,64,256]{2,1,0:T(8,128)S(1)} %copy-done.3, f32[16,64,256]{2,0,1:T(8,128)S(1)} %fusion.26), kind=kOutput, calls=%fused_computation.93 | convolution fusion | flops 1610874880 | bytes 12582912
  225.0 12.9 %fusion.5 = f32[16,8,64,256]{3,2,1,0:T(8,128)} fusion(f32[16,8,64,256]{3,2,1,0:T(8,128)} %bitcast.134, f32[16,8,64,256]{3,2,1,0:T(8,128)} %bitcast.130, f32[16,256]{1,0:T(8,128)S(1)} %bitcast_reduce_fusion.1), kind=kLoop, calls=%fused_computation.16 | loop fusion | flops 4194304 | bytes 25182208 | tf_op jit(solution)/shard_map/mul | solution.py:44
  237.9 11.0 %fusion = f32[32,64,256,1]{2,0,3,1:T(8,128)S(1)} fusion(f32[16,8,64,256]{3,2,1,0:T(8,128)} %fusion.5, s32[16,8]{1,0:T(8,128)S(1)} %copy.61), kind=kOutput, calls=%fused_computation.9 | convolution fusion | flops 805310464 | bytes 10486272 | tf_op jit(solution)/shard_map/bkp,bkjs->pjs/dot_general | solution.py:49
  248.9 1.1 fusion.16
  250.1 1.6 copy.71
  251.6 3.6 all-to-all-start.3
  255.2 0.1 eq.86
  255.3 26.4 %all-to-all-done.3 = f32[16,64,256]{2,1,0:T(8,128)S(1)} async-done(((f32[16,64,256]{2,1,0:T(8,128)}), f32[16,64,256]{2,1,0:T(8,128)S(1)}, u32[]{:S(2)}, u32[]{:S(2)}) %all-to-all-start.3) | async-done | bytes 1048608 | tf_op jit(solution)/shard_map/all_to_all | solution.py:11
  281.7 1.2 fusion.24
  282.9 1.6 copy.73
  284.5 101.0 %all-reduce.3.cloned.1.call-done = (f32[1,16,8,64,64]{3,4,2,1,0:T(8,128)}, f32[1,16,8,64,64]{3,4,2,1,0:T(8,128)}) async-done(((f32[1,16,8,64,64]{3,4,2,1,0:T(8,128)}, f32[1,16,8,64,64]{3,4,2,1,0:T(8,128)}), (f32[1,16,8,64,64]{3,4,2,1,0:T(8,128)}, f32[1,16,8,64,64]{3,4,2,1,0:T(8,128)})) %all-reduce.3.cloned.1.call-update) | async-done | bytes 4194320 | tf_op jit(solution)/shard_map/psum | solution.py:64
  385.5 8.8 %maximum_multiply_fusion = f32[2,16,8,64,64]{3,4,2,1,0:T(8,128)} fusion(f32[1,16,8,64,64]{3,4,2,1,0:T(8,128)} %get-tuple-element.15, f32[1,16,8,64,64]{3,4,2,1,0:T(8,128)} %get-tuple-element.16), kind=kLoop, calls=%fused_computation.8 | loop fusion | flops 2097152 | bytes 8388608 | tf_op jit(solution)/shard_map/div | solution.py:67
  394.3 8.7 %copy.74 = f32[2,16,8,64,64]{4,3,2,1,0:T(8,128)} copy(f32[2,16,8,64,64]{3,4,2,1,0:T(8,128)} %maximum_multiply_fusion) | data formatting | bytes 8388608
  (23 shorter events, 0.2 us)
Async XLA Ops:
  7.2 1.3 copy-start
  10.0 32.9 %all-to-all-start = ((f32[16,64,256]{2,1,0:T(8,128)}), f32[16,64,256]{2,1,0:T(8,128)S(1)}, u32[]{:S(2)}, u32[]{:S(2)}) async-start(f32[16,64,256]{2,1,0:T(8,128)} %gather_fusion), calls=%async_computation | async-start | bytes 2097152 | tf_op jit(solution)/shard_map/all_to_all | solution.py:28
  73.8 30.6 %all-to-all-start.1 = ((f32[16,64,256]{2,1,0:T(8,128)}), f32[16,64,256]{2,1,0:T(8,128)S(1)}, u32[]{:S(2)}, u32[]{:S(2)}) async-start(f32[16,64,256]{2,1,0:T(8,128)} %gather_fusion.4), calls=%async_computation.1 | async-start | bytes 2097152 | tf_op jit(solution)/shard_map/all_to_all | solution.py:28
  86.4 5.4 %copy-start.5 = (s32[2,16,8]{1,2,0:T(8,128)S(1)}, s32[2,16,8]{1,2,0:T(8,128)}, u32[]{:S(2)}) copy-start(s32[2,16,8]{1,2,0:T(8,128)} %param.10) | copy-start | bytes 3076
  120.1 13.4 %copy-start.2 = (f32[16,8,64,64]{2,3,1,0:T(8,128)S(1)}, f32[16,8,64,64]{2,3,1,0:T(8,128)}, u32[]{:S(2)}) copy-start(f32[16,8,64,64]{2,3,1,0:T(8,128)} %copy.64) | copy-start | bytes 6291460
  120.1 13.4 %copy-start.4 = (f32[16,64,256]{2,1,0:T(8,128)S(1)}, f32[16,64,256]{2,1,0:T(8,128)}, u32[]{:S(2)}) copy-start(f32[16,64,256]{2,1,0:T(8,128)} %param.11) | copy-start | bytes 3145732
  168.2 31.1 %all-to-all-start.2 = ((f32[16,64,256]{2,1,0:T(8,128)}), f32[16,64,256]{2,1,0:T(8,128)}, u32[]{:S(2)}, u32[]{:S(2)}) async-start(f32[16,64,256]{2,1,0:T(8,128)} %copy.66), calls=%async_computation.2 | async-start | bytes 2097152 | tf_op jit(solution)/shard_map/all_to_all | solution.py:11
  172.7 212.8 %all-reduce.3.cloned.1.call-start = ((), (), s32[]{:S(2)}) async-start(), calls=%async_computation.4 | async-start | bytes 16777216 | tf_op jit(solution)/shard_map/psum | solution.py:64
  178.3 23.4 %copy-start.3 = (f32[16,64,256]{2,1,0:T(8,128)S(1)}, f32[16,64,256]{2,1,0:T(8,128)}, u32[]{:S(2)}) copy-start(f32[16,64,256]{2,1,0:T(8,128)} %get-tuple-element.32) | copy-start | bytes 3145732
  251.6 30.1 %all-to-all-start.3 = ((f32[16,64,256]{2,1,0:T(8,128)}), f32[16,64,256]{2,1,0:T(8,128)S(1)}, u32[]{:S(2)}, u32[]{:S(2)}) async-start(f32[16,64,256]{2,1,0:T(8,128)} %copy.71), calls=%async_computation.3 | async-start | bytes 2097152 | tf_op jit(solution)/shard_map/all_to_all | solution.py:11
  385.5 17.5 %copy-start.1 = (f32[16,64,256]{2,1,0:T(8,128)S(1)}, f32[16,64,256]{2,1,0:T(8,128)}, u32[]{:S(2)}) copy-start(f32[16,64,256]{2,1,0:T(8,128)} %param.6) | copy-start | bytes 3145732
Sparse Core Ops, SparseCore 0:
  214.0 171.4 all-reduce.2
where the time goes:
time: 417 us; the launch traced here: 410 us
  waiting for transfers between devices  174 us (42%)
  matrix products  98.5 us (24%)
  local copies, waits for them, and re-layouts  55.4 us (13%)
  other arithmetic  49.2 us (12%)
  starting transfers between devices  18.5 us (4%)
  between operations  14.4 us (3%)
    psum x1, waiting for transfers between devices, per_device(): flow_part = lax.psum(flow_part, 'dp')  101 us
    all_to_all x2, waiting for transfers between devices, per_device(): lax.all_to_all(outgoing, 'region', split_axis=0, concat_axis=0, tiled=True)  37.2 us
    all_to_all x2, waiting for transfers between devices, send_home(): lax.all_to_all(slot_gradient, 'region', split_axis=0, concat_axis=0, tile...  35.8 us
    dot_general x2, matrix products, per_device(): jnp.einsum('bkij,bkjs->bis', weights[level], exponent, precision=maximum_...  26.7 us
    mul x2, other arithmetic, per_device(): jnp.einsum('bkij,bis->bkjs', weights[level], ratio, precision=maximum_value)  24.8 us
    dot_general x2, matrix products, per_device(): jnp.einsum('bis,bkjs->bkij', ratio, exponent, precision=maximum_value)  23.9 us
    dot_general x2, matrix products, per_device(): jnp.einsum('bkp,bkjs->pjs', chooser, grad_chosen, precision=maximum_value)  21.9 us
    unnamed x2, matrix products  20.2 us
  transfers between devices with their start and end apart: 5, of which 5 were waited for; matrix products, arithmetic and copies ran while one was open for 18% of the time, Pallas kernels for 0%

commit v1 on v0

v1 whole, which is shorter than its diff:
```python
import functools

import jax
import jax.numpy as jnp
from jax import lax
from jax.experimental import pallas as pl
from jax.experimental.pallas import tpu as pltpu
from jax.sharding import PartitionSpec as P

F32, BF16 = jnp.float32, jnp.bfloat16
SMEM = pl.BlockSpec(memory_space=pltpu.SMEM)
VMEM = pl.BlockSpec(memory_space=pltpu.VMEM)
ANY = pl.BlockSpec(memory_space=pl.ANY)
LIMIT = 56 * 2**20


def params():
    return pltpu.CompilerParams(vmem_limit_bytes=LIMIT)


def cost(flops, nbytes, exps=0):
    return pl.CostEstimate(flops=flops, bytes_accessed=nbytes, transcendentals=exps)


def halves(x):
    high = x.astype(BF16)
    return high, (x - high.astype(F32)).astype(BF16)


def dot(a, b, dims):
    return lax.dot_general(a, b, (dims, ((), ())), preferred_element_type=F32)


def make_prods(level, kids, taken, prods, tops):
    count = prods.shape[0]

    def step(p, _):
        at = (level * count + p) * 2
        value = taken[kids[at]] + taken[kids[at + 1]]
        prods[p] = value
        tops[p] = jnp.max(value, axis=0, keepdims=True)
        return _

    lax.fori_loop(0, count, step, 0, unroll=2)


def chosen_ids(level, lists, b, blocks, kinds):
    return [lists[(level * blocks + b) * kinds + k] for k in range(kinds)]


def shift_of(ids, tops):
    shift = tops[ids[0]]
    for i in ids[1:]:
        shift = jnp.maximum(shift, tops[i])
    return shift


def expo_of(ids, prods, shift):
    return jnp.concatenate([jnp.exp(prods[i] - shift) for i in ids], axis=0)


def wide_weights(weights, b):
    return jnp.concatenate([weights[b, k] for k in range(weights.shape[1])], axis=1)


def totals_of(w_high, w_low, e_high, e_low):
    rows = w_high.shape[0]
    both = dot(jnp.concatenate([w_high, w_low], axis=0), e_high, ((1,), (0,)))
    return both[:rows] + both[rows:] + dot(w_high, e_low, ((1,), (0,)))


def flow_of(r_high, r_low, e_high, e_low):
    rows = r_high.shape[0]
    both = dot(jnp.concatenate([r_high, r_low], axis=0), e_high, ((1,), (1,)))
    return both[:rows] + both[rows:] + dot(r_high, e_low, ((1,), (1,)))


def chosen_grad(w_high, w_low, r_high, r_low, expo):
    left = jnp.concatenate([w_high, w_low, w_high], axis=0)
    right = jnp.concatenate([r_high, r_high, r_low], axis=0)
    return dot(left, right, ((0,), (0,))) * expo


def add_chosen(ids, grad, prod_grad):
    rows = prod_grad.shape[1]
    for k, i in enumerate(ids):
        prod_grad[i] += grad[k * rows : (k + 1) * rows]


def to_slots(level, kids, prod_grad, slot_grad):
    slot_grad[...] = jnp.zeros_like(slot_grad)
    count = prod_grad.shape[0]

    def step(p, _):
        at = (level * count + p) * 2
        value = prod_grad[p]
        slot_grad[kids[at]] += value
        slot_grad[kids[at + 1]] += value
        return _

    lax.fori_loop(0, count, step, 0)


def home(level, group_ids, sent, grad):
    slots = sent.shape[0]
    grad[...] = jnp.zeros_like(grad)

    def step(i, _):
        grad[group_ids[level * slots + i]] += sent[i]
        return _

    lax.fori_loop(0, slots, step, 0)


def pick_kernel(level, group_ids, source, out, sems):
    slots = out.shape[0]
    copies = [
        pltpu.make_async_copy(
            source.at[group_ids[level * slots + i]], out.at[i], sems.at[i]
        )
        for i in range(slots)
    ]
    for c in copies:
        c.start()
    for c in copies:
        c.wait()


def forward_kernel(level, group_ids, kids, lists, taken, weights, outgoing, totals, prods, tops, level_out):
    blocks, kinds = weights.shape[:2]
    make_prods(level, kids, taken, prods, tops)

    def step(b, _):
        ids = chosen_ids(level, lists, b, blocks, kinds)
        shift = shift_of(ids, tops)
        e = halves(expo_of(ids, prods, shift))
        w = halves(wide_weights(weights, b))
        total = totals_of(*w, *e)
        totals[b] = total
        level_out[b] = shift + jnp.log(total)
        return _

    lax.fori_loop(0, blocks, step, 0, unroll=2)
    slots = outgoing.shape[0]

    def send(i, _):
        outgoing[i] = level_out[group_ids[(level + 1) * slots + i]]
        return _

    lax.fori_loop(0, slots, send, 0)


def top_kernel(level, scale, kids, lists, taken, weights, cotangent, top, slot_grad, flow, prods, tops, prod_grad):
    blocks, kinds = weights.shape[:2]
    make_prods(level, kids, taken, prods, tops)
    prod_grad[...] = jnp.zeros_like(prod_grad)

    def step(b, _):
        ids = chosen_ids(level, lists, b, blocks, kinds)
        shift = shift_of(ids, tops)
        expo = expo_of(ids, prods, shift)
        e = halves(expo)
        w = halves(wide_weights(weights, b))
        total = totals_of(*w, *e)
        top[b] = shift + jnp.log(total)
        r = halves(cotangent[b] / total)
        flow[b] = flow_of(*r, *e) * scale
        add_chosen(ids, chosen_grad(*w, *r, expo), prod_grad)
        return _

    lax.fori_loop(0, blocks, step, 0, unroll=2)
    to_slots(level, kids, prod_grad, slot_grad)


def flow_kernel(level, scale, group_ids, kids, lists, taken, totals, sent, ratio, flow, prods, tops, grad):
    blocks = totals.shape[0]
    kinds = flow.shape[2] // flow.shape[1]
    home(level + 1, group_ids, sent, grad)
    make_prods(level, kids, taken, prods, tops)

    def step(b, _):
        ids = chosen_ids(level, lists, b, blocks, kinds)
        e = halves(expo_of(ids, prods, shift_of(ids, tops)))
        value = grad[b] / totals[b]
        ratio[b] = value
        flow[b] = flow_of(*halves(value), *e) * scale
        return _

    lax.fori_loop(0, blocks, step, 0, unroll=2)


def slots_kernel(level, kids, lists, taken, weights, ratio, slot_grad, prods, tops, prod_grad):
    blocks, kinds = weights.shape[:2]
    make_prods(level, kids, taken, prods, tops)
    prod_grad[...] = jnp.zeros_like(prod_grad)

    def step(b, _):
        ids = chosen_ids(level, lists, b, blocks, kinds)
        expo = expo_of(ids, prods, shift_of(ids, tops))
        w = halves(wide_weights(weights, b))
        add_chosen(ids, chosen_grad(*w, *halves(ratio[b]), expo), prod_grad)
        return _

    lax.fori_loop(0, blocks, step, 0, unroll=2)
    to_slots(level, kids, prod_grad, slot_grad)


def home_kernel(level, group_ids, sent, grad):
    home(level, group_ids, sent, grad)


def unfold_kernel(flow, *rest):
    out = rest[-1]
    rows = flow.shape[1]

    for k in range(out.shape[1]):
        out[0, k] = flow[0, :, k * rows : (k + 1) * rows]


def unfold(level, levels, kinds, flow, base=None):
    blocks, rows, _ = flow.shape
    given = [] if base is None else [base]
    return pl.pallas_call(
        unfold_kernel,
        grid=(blocks,),
        out_shape=jax.ShapeDtypeStruct((levels, blocks, kinds, rows, rows), F32),
        in_specs=[pl.BlockSpec((1, rows, kinds * rows), lambda b: (b, 0, 0))] + [ANY] * len(given),
        out_specs=pl.BlockSpec((None, 1, kinds, rows, rows), lambda b: (level, b, 0, 0, 0)),
        input_output_aliases={1: 0} if given else {},
        compiler_params=params(),
        cost_estimate=cost(0, 6 * 2**20),
        name="unfold",
    )(flow, *given)


def swap(x):
    return lax.all_to_all(x, "region", split_axis=0, concat_axis=0, tiled=True)


def per_device(leaves, weights, groups, prod_kids, sum_kids, cotangent):
    levels, blocks, kinds, rows, _ = weights.shape
    columns = leaves.shape[2]
    slots = groups.shape[1] * groups.shape[3]
    count = prod_kids.shape[1]
    scale = 1.0 / (columns * lax.axis_size("dp"))
    group_ids, kids, lists = groups.reshape(-1), prod_kids.reshape(-1), sum_kids.reshape(-1)

    def shape(*dims):
        return jax.ShapeDtypeStruct(dims, F32)

    taken_like, level_like = shape(slots, rows, columns), shape(blocks, rows, columns)
    flow_like = shape(blocks, rows, kinds * rows)
    prod_scratch = [
        pltpu.VMEM((count, rows, columns), F32),
        pltpu.VMEM((count, 1, columns), F32),
    ]
    prod_grad = pltpu.VMEM((count, rows, columns), F32)
    macs = blocks * rows * rows * kinds * columns
    expos = blocks * kinds * rows * columns
    mib = 2**20

    def call(kernel, outs, scratch, amount, *args, specs, name, out_specs=None):
        return pl.pallas_call(
            kernel,
            out_shape=outs,
            in_specs=specs,
            out_specs=out_specs or jax.tree.map(lambda _: VMEM, outs),
            scratch_shapes=scratch,
            compiler_params=params(),
            cost_estimate=amount,
            name=name,
        )(*args)

    outgoing = call(
        functools.partial(pick_kernel, 0), taken_like, [pltpu.SemaphoreType.DMA((slots,))],
        cost(0, 2 * mib), group_ids, leaves, specs=[SMEM, ANY], out_specs=ANY, name="pick",
    )
    kept = []
    for level in range(levels - 1):
        taken = swap(outgoing)
        outgoing, totals = call(
            functools.partial(forward_kernel, level), (taken_like, level_like),
            prod_scratch + [pltpu.VMEM((blocks, rows, columns), F32)],
            cost(24 * macs, 8 * mib, expos), group_ids, kids, lists, taken, weights[level],
            specs=[SMEM] * 3 + [VMEM] * 2, name="forward",
        )
        kept.append((taken, totals))
    level = levels - 1
    taken = swap(outgoing)
    top, slot_grad, flow = call(
        functools.partial(top_kernel, level, scale), (level_like, taken_like, flow_like),
        prod_scratch + [prod_grad], cost(72 * macs, 12 * mib, expos),
        kids, lists, taken, weights[level], cotangent,
        specs=[SMEM] * 2 + [VMEM] * 3, name="top",
    )
    sent = swap(slot_grad)
    flow = lax.psum(flow, "dp")
    weight_flow = unfold(level, levels, kinds, flow)
    for level in reversed(range(levels - 1)):
        taken, totals = kept[level]
        ratio, part = call(
            functools.partial(flow_kernel, level, scale), (level_like, flow_like),
            prod_scratch + [pltpu.VMEM((blocks, rows, columns), F32)],
            cost(24 * macs, 8 * mib, expos), group_ids, kids, lists, taken, totals, sent,
            specs=[SMEM] * 3 + [VMEM] * 3, name="flow",
        )
        part, flow = lax.optimization_barrier((part, flow))
        slot_grad = call(
            functools.partial(slots_kernel, level), taken_like, prod_scratch + [prod_grad],
            cost(24 * macs, 8 * mib, expos), kids, lists, taken, weights[level], ratio,
            specs=[SMEM] * 2 + [VMEM] * 3, name="slots",
        )
        sent = swap(slot_grad)
        flow = lax.psum(part, "dp")
        weight_flow = unfold(level, levels, kinds, flow, weight_flow)
    leaf_grad = call(
        functools.partial(home_kernel, 0), level_like, [], cost(0, 2 * mib), group_ids, sent,
        specs=[SMEM, VMEM], name="home",
    )
    return top, leaf_grad, weight_flow


def solution(mesh):
    placed = (
        P("region", None, "dp"),
        P(None, "region", None, None, None),
        P(None, None, "region", None),
        P(None, "region", None),
        P(None, "region", None),
        P("region", None, "dp"),
    )
    return jax.shard_map(
        per_device,
        mesh=mesh,
        in_specs=placed,
        out_specs=(
            P("region", None, "dp"),
            P("region", None, "dp"),
            P(None, "region", None, None, None),
        ),
        check_vma=False,
    )
```

time: 417 us -> 299 us (0.72); the launches traced: 410 us -> 298 us
  matrix products: 98.5 us -> 0 us
  Pallas kernels: 0 us -> 97.4 us
  other arithmetic: 49.2 us -> 0 us
  waiting for transfers between devices: 174 us -> 127 us
  local copies, waits for them, and re-layouts: 55.4 us -> 14.4 us
  blocking collectives: 0 us -> 30.8 us
    pallas_call x0 -> x8, Pallas kernels: none -> 97.4 us  [the longest x6 76.8 us: call(): pl.pallas_call(kernel, out_shape=outs, in_specs=specs, out_specs=out_spec...]
    dot_general x10 -> x0, matrix products: 78.3 us -> none  [the longest x2 26.7 us: per_device(): jnp.einsum('bkij,bkjs->bis', weights[level], exponent, precision=maximum_...]
    psum x1 -> x2, waiting for transfers between devices: 101 us -> 67.8 us  [the longest x1 39.7 us: per_device(): flow = lax.psum(flow, 'dp')]
    all_to_all x0 -> x1, blocking collectives: none -> 30.8 us  [swap(): return lax.all_to_all(x, 'region', split_axis=0, concat_axis=0, tiled=True)]
    mul x2 -> x0, other arithmetic: 24.8 us -> none  [per_device(): jnp.einsum('bkij,bis->bkjs', weights[level], ratio, precision=maximum_value)]
    unnamed x2 -> x0, matrix products: 20.2 us -> none
    gather x8 -> x0, local copies, waits for them, and re-layouts: 20 us -> none  [the longest x2 8.81 us: per_device(): chosen = prods[sum_kids[level]]]
    all_to_all x4 -> x3, waiting for transfers between devices: 73 us -> 58.5 us  [swap(): return lax.all_to_all(x, 'region', split_axis=0, concat_axis=0, tiled=True)]
  transfers between devices with their start and end apart: 5 -> 5, of which waited for: 5 -> 5; matrix products, arithmetic and copies ran while one was open for 18% -> 3% of each run, Pallas kernels for 0% -> 10%
where the time goes in v1:
time: 299 us; the launch traced here: 298 us
  waiting for transfers between devices  127 us (42%)
  Pallas kernels  97.4 us (33%)
  blocking collectives  30.8 us (10%)
  starting transfers between devices  14.6 us (5%)
  local copies, waits for them, and re-layouts  14.4 us (5%)
  between operations  14.1 us (5%)
    pallas_call x6, Pallas kernels, call(): pl.pallas_call(kernel, out_shape=outs, in_specs=specs, out_specs=out_spec...  76.8 us
    all_to_all x3, waiting for transfers between devices, swap(): return lax.all_to_all(x, 'region', split_axis=0, concat_axis=0, tiled=True)  58.5 us
    psum x1, waiting for transfers between devices, per_device(): flow = lax.psum(flow, 'dp')  39.7 us
    all_to_all x1, blocking collectives, swap(): return lax.all_to_all(x, 'region', split_axis=0, concat_axis=0, tiled=True)  30.8 us
    psum x1, waiting for transfers between devices, per_device(): flow = lax.psum(part, 'dp')  28.2 us
    pallas_call x2, Pallas kernels, unfold(): pl.pallas_call(unfold_kernel, grid=(blocks,), out_shape=jax.ShapeDtypeStr...  20.6 us
    all_to_all x3, starting transfers between devices, swap(): return lax.all_to_all(x, 'region', split_axis=0, concat_axis=0, tiled=True)  14.5 us
    squeeze x1, local copies, waits for them, and re-layouts, per_device(): weights[level]  8.46 us
  transfers between devices with their start and end apart: 5, of which 5 were waited for; matrix products, arithmetic and copies ran while one was open for 3% of the time, Pallas kernels for 10%

profile of v1, /device:TPU:0, one launch (start us, length us, event | category | flops | bytes accessed | tf_op | source)
XLA Modules:
  0.0 298.4 jit_solution(9026467868074812479)
XLA Ops:
  7.2 0.0 copy-start.3
  7.2 0.0 copy-start.4
  7.2 0.8 copy.14
  8.0 0.7 reshape.17.group_ids
  8.6 33.7 %pick.1 = f32[16,64,256]{2,1,0:T(8,128)} custom-call(s32[32]{0:T(128)} %reshape.17.group_ids, f32[16,64,256]{2,1,0:T(8,128)} %source.1), custom_call_target="tpu_custom_call" | custom-call | bytes 2097152 | tf_op jit(solution)/shard_map/pick/pallas_call | solution.py:263
  42.3 6.3 %all-to-all-start = ((f32[16,64,256]{2,1,0:T(8,128)}), f32[16,64,256]{2,1,0:T(8,128)S(1)}, u32[]{:S(2)}, u32[]{:S(2)}) async-start(f32[16,64,256]{2,1,0:T(8,128)} %pick.1), calls=%async_computation | async-start | bytes 2097152 | tf_op jit(solution)/shard_map/all_to_all | solution.py:237
  48.6 0.0 copy-done.3
  48.7 0.1 copy.13
  48.7 0.7 reshape.16.lists
  49.4 0.0 copy-done.4
  49.4 0.1 copy.12
  49.5 0.7 reshape.15.kids
  50.2 8.5 %slice_bitcast_fusion = (f32[16,8,64,64]{3,2,1,0:T(8,128)}, f32[16,8,64,64]{3,2,1,0:T(8,128)}) fusion(f32[2,16,8,64,64]{4,3,2,1,0:T(8,128)} %param.7), kind=kLoop, calls=%fused_computation | loop fusion | bytes 8388608 | tf_op jit(solution)/shard_map/squeeze | solution.py:293
  58.7 16.5 %all-to-all-done.taken = f32[16,64,256]{2,1,0:T(8,128)S(1)} async-done(((f32[16,64,256]{2,1,0:T(8,128)}), f32[16,64,256]{2,1,0:T(8,128)S(1)}, u32[]{:S(2)}, u32[]{:S(2)}) %all-to-all-start) | async-done | bytes 1048608 | tf_op jit(solution)/shard_map/all_to_all | solution.py:237
  75.2 0.0 copy-start.1
  75.2 1.0 copy-done.1
  76.2 8.0 %forward.1 = (f32[16,64,256]{2,1,0:T(8,128)}, f32[16,64,256]{2,1,0:T(8,128)}) custom-call(s32[32]{0:T(128)} %reshape.17.group_ids, s32[128]{0:T(128)} %reshape.15.kids, s32[256]{0:T(256)} %reshape.16.lists, f32[16,64,256]{2,1,0:T(8,128)} %copy-done.1, f32[16,8,64,64]{3,2,1,0:T(8,128)} %get-tuple-element.20.weights), custom_call_target="tpu_custom_call" | custom-call | flops 3221225472 | bytes 8388608 | tf_op jit(solution)/shard_map/forward/pallas_call | solution.py:263
  84.2 30.8 %all_to_all.20.taken = f32[16,64,256]{2,1,0:T(8,128)} all-to-all(f32[16,64,256]{2,1,0:T(8,128)} %get-tuple-element.11), channel_id=1, replica_groups=mesh['dp'=4,'region'=8] {'region'}, dimensions={0} | all-to-all | bytes 2097152 | tf_op jit(solution)/shard_map/all_to_all | solution.py:237
  115.0 14.6 %top.1 = (f32[16,64,256]{2,1,0:T(8,128)}, f32[16,64,256]{2,1,0:T(8,128)}, f32[16,64,512]{2,1,0:T(8,128)}) custom-call(s32[128]{0:T(128)} %reshape.15.kids, s32[256]{0:T(256)} %reshape.16.lists, f32[16,64,256]{2,1,0:T(8,128)} %all_to_all.20.taken, f32[16,8,64,64]{3,2,1,0:T(8,128)} %get-tuple-element.19.weights, f32[16,64,256]{2,1,0:T(8,128)} %cotangent.1), custom_call_target="tpu_custom_call" | custom-call | flops 9663676416 | bytes 12582912 | tf_op jit(solution)/shard_map/top/pallas_call | solution.py:263
  129.6 3.6 %all-to-all-start.2 = ((f32[16,64,256]{2,1,0:T(8,128)}), f32[16,64,256]{2,1,0:T(8,128)S(1)}, u32[]{:S(2)}, u32[]{:S(2)}) async-start(f32[16,64,256]{2,1,0:T(8,128)} %get-tuple-element.14), calls=%async_computation.2 | async-start | bytes 2097152 | tf_op jit(solution)/shard_map/all_to_all | solution.py:237
  133.2 0.0 all-reduce.3.cloned.1.call-start
  133.2 0.7 all-reduce.3.cloned.1.call-update
  133.9 0.0 all-reduce.5.cloned.1.call-start
  134.0 25.7 %all-to-all-done.2.sent = f32[16,64,256]{2,1,0:T(8,128)S(1)} async-done(((f32[16,64,256]{2,1,0:T(8,128)}), f32[16,64,256]{2,1,0:T(8,128)S(1)}, u32[]{:S(2)}, u32[]{:S(2)}) %all-to-all-start.2) | async-done | bytes 1048608 | tf_op jit(solution)/shard_map/all_to_all | solution.py:237
  159.7 0.0 copy-start.2
  159.7 1.0 copy-done.2
  160.7 7.9 %flow.1 = (f32[16,64,256]{2,1,0:T(8,128)}, f32[16,64,512]{2,1,0:T(8,128)}) custom-call(s32[32]{0:T(128)} %reshape.17.group_ids, s32[128]{0:T(128)} %reshape.15.kids, s32[256]{0:T(256)} %reshape.16.lists, f32[16,64,256]{2,1,0:T(8,128)} %copy-done.1, f32[16,64,256]{2,1,0:T(8,128)} %get-tuple-element.13.totals, f32[16,64,256]{2,1,0:T(8,128)} %copy-done.2), custom_call_target="tpu_custom_call" | custom-call | flops 3221225472 | bytes 8388608 | tf_op jit(solution)/shard_map/flow/pallas_call | solution.py:263
  168.5 39.7 %all-reduce.3.cloned.1.call-done.flow = f32[16,64,512]{2,1,0:T(8,128)} async-done(((f32[16,64,512]{2,1,0:T(8,128)}), f32[16,64,512]{2,1,0:T(8,128)}) %all-reduce.3.cloned.1.call-update) | async-done | bytes 2097168 | tf_op jit(solution)/shard_map/psum | solution.py:297
  208.2 0.0 all-reduce.5.cloned.1.call-update
  208.2 10.2 %slots.1 = f32[16,64,256]{2,1,0:T(8,128)} custom-call(s32[128]{0:T(128)} %reshape.15.kids, s32[256]{0:T(256)} %reshape.16.lists, f32[16,64,256]{2,1,0:T(8,128)} %copy-done.1, f32[16,8,64,64]{3,2,1,0:T(8,128)} %get-tuple-element.20.weights, f32[16,64,256]{2,1,0:T(8,128)} %get-tuple-element.15.ratio), custom_call_target="tpu_custom_call" | custom-call | flops 3221225472 | bytes 8388608 | tf_op jit(solution)/shard_map/slots/pallas_call | solution.py:263
  218.4 4.6 %all-to-all-start.3 = ((f32[16,64,256]{2,1,0:T(8,128)}), f32[16,64,256]{2,1,0:T(8,128)S(1)}, u32[]{:S(2)}, u32[]{:S(2)}) async-start(f32[16,64,256]{2,1,0:T(8,128)} %slots.1), calls=%async_computation.3 | async-start | bytes 2097152 | tf_op jit(solution)/shard_map/all_to_all | solution.py:237
  223.0 10.3 %unfold.2.rest_0_ = f32[2,16,8,64,64]{4,3,2,1,0:T(8,128)} custom-call(f32[16,64,512]{2,1,0:T(8,128)} %all-reduce.3.cloned.1.call-done.flow), custom_call_target="tpu_custom_call" | custom-call | bytes 6291456 | tf_op jit(solution)/shard_map/unfold/pallas_call | solution.py:223
  233.4 16.3 %all-to-all-done.3.sent = f32[16,64,256]{2,1,0:T(8,128)S(1)} async-done(((f32[16,64,256]{2,1,0:T(8,128)}), f32[16,64,256]{2,1,0:T(8,128)S(1)}, u32[]{:S(2)}, u32[]{:S(2)}) %all-to-all-start.3) | async-done | bytes 1048608 | tf_op jit(solution)/shard_map/all_to_all | solution.py:237
  249.6 0.0 copy-start
  249.6 1.0 copy-done
  250.6 2.5 home.1
  253.1 28.2 %all-reduce.5.cloned.1.call-done.flow = f32[16,64,512]{2,1,0:T(8,128)} async-done(((f32[16,64,512]{2,1,0:T(8,128)}), f32[16,64,512]{2,1,0:T(8,128)}) %all-reduce.5.cloned.1.call-update) | async-done | bytes 2097168 | tf_op jit(solution)/shard_map/psum | solution.py:314
  281.3 10.3 %unfold.3 = f32[2,16,8,64,64]{4,3,2,1,0:T(8,128)} custom-call(f32[16,64,512]{2,1,0:T(8,128)} %all-reduce.5.cloned.1.call-done.flow, f32[2,16,8,64,64]{4,3,2,1,0:T(8,128)} %unfold.2.rest_0_), custom_call_target="tpu_custom_call", output_to_operand_aliasing={{}: (1, {})} | custom-call | bytes 6291456 | tf_op jit(solution)/shard_map/unfold/pallas_call | solution.py:223
Async XLA Ops:
  7.2 41.5 %copy-start.3 = (s32[2,16,8]{1,2,0:T(8,128)S(1)}, s32[2,16,8]{1,2,0:T(8,128)}, u32[]{:S(2)}) copy-start(s32[2,16,8]{1,2,0:T(8,128)} %param.10) | copy-start | bytes 3076
  7.2 42.2 %copy-start.4 = (s32[2,32,2]{1,2,0:T(2,128)S(1)}, s32[2,32,2]{1,2,0:T(2,128)}, u32[]{:S(2)}) copy-start(s32[2,32,2]{1,2,0:T(2,128)} %param.9) | copy-start | bytes 1540
  42.3 32.9 %all-to-all-start = ((f32[16,64,256]{2,1,0:T(8,128)}), f32[16,64,256]{2,1,0:T(8,128)S(1)}, u32[]{:S(2)}, u32[]{:S(2)}) async-start(f32[16,64,256]{2,1,0:T(8,128)} %pick.1), calls=%async_computation | async-start | bytes 2097152 | tf_op jit(solution)/shard_map/all_to_all | solution.py:237
  75.2 1.0 copy-start.1
  129.6 30.1 %all-to-all-start.2 = ((f32[16,64,256]{2,1,0:T(8,128)}), f32[16,64,256]{2,1,0:T(8,128)S(1)}, u32[]{:S(2)}, u32[]{:S(2)}) async-start(f32[16,64,256]{2,1,0:T(8,128)} %get-tuple-element.14), calls=%async_computation.2 | async-start | bytes 2097152 | tf_op jit(solution)/shard_map/all_to_all | solution.py:237
  133.2 75.0 %all-reduce.3.cloned.1.call-start = ((), (), s32[]{:S(2)}) async-start(), calls=%async_computation.4 | async-start | bytes 4194304 | tf_op jit(solution)/shard_map/psum | solution.py:297
  133.9 147.4 %all-reduce.5.cloned.1.call-start = ((), (), s32[]{:S(2)}) async-start(), calls=%async_computation.5 | async-start | bytes 4194304 | tf_op jit(solution)/shard_map/psum | solution.py:314
  159.7 1.0 copy-start.2
  218.4 31.2 %all-to-all-start.3 = ((f32[16,64,256]{2,1,0:T(8,128)}), f32[16,64,256]{2,1,0:T(8,128)S(1)}, u32[]{:S(2)}, u32[]{:S(2)}) async-start(f32[16,64,256]{2,1,0:T(8,128)} %slots.1), calls=%async_computation.3 | async-start | bytes 2097152 | tf_op jit(solution)/shard_map/all_to_all | solution.py:237
  249.6 1.0 copy-start
Sparse Core Ops, SparseCore 0:
  137.1 71.0 all-reduce.2
  211.6 69.6 all-reduce.4

commit v2 on v1

--- a/solution.py
+++ b/solution.py
@@ -126,9 +126,12 @@
         c.wait()
 
 
-def forward_kernel(level, group_ids, kids, lists, taken, weights, outgoing, totals, prods, tops, level_out):
+def forward_kernel(level, group_ids, kids, lists, taken, all_weights, outgoing, totals, prods, tops, level_out, weights, sem):
+    arriving = pltpu.make_async_copy(all_weights.at[level], weights, sem)
+    arriving.start()
     blocks, kinds = weights.shape[:2]
     make_prods(level, kids, taken, prods, tops)
+    arriving.wait()
 
     def step(b, _):
         ids = chosen_ids(level, lists, b, blocks, kinds)
@@ -150,10 +153,13 @@
     lax.fori_loop(0, slots, send, 0)
 
 
-def top_kernel(level, scale, kids, lists, taken, weights, cotangent, top, slot_grad, flow, prods, tops, prod_grad):
+def top_kernel(level, scale, kids, lists, taken, all_weights, cotangent, top, slot_grad, flow, prods, tops, prod_grad, weights, sem):
+    arriving = pltpu.make_async_copy(all_weights.at[level], weights, sem)
+    arriving.start()
     blocks, kinds = weights.shape[:2]
     make_prods(level, kids, taken, prods, tops)
     prod_grad[...] = jnp.zeros_like(prod_grad)
+    arriving.wait()
 
     def step(b, _):
         ids = chosen_ids(level, lists, b, blocks, kinds)
@@ -189,10 +195,13 @@
     lax.fori_loop(0, blocks, step, 0, unroll=2)
 
 
-def slots_kernel(level, kids, lists, taken, weights, ratio, slot_grad, prods, tops, prod_grad):
+def slots_kernel(level, kids, lists, taken, all_weights, ratio, slot_grad, prods, tops, prod_grad, weights, sem):
+    arriving = pltpu.make_async_copy(all_weights.at[level], weights, sem)
+    arriving.start()
     blocks, kinds = weights.shape[:2]
     make_prods(level, kids, taken, prods, tops)
     prod_grad[...] = jnp.zeros_like(prod_grad)
+    arriving.wait()
 
     def step(b, _):
         ids = chosen_ids(level, lists, b, blocks, kinds)
@@ -209,32 +218,70 @@
     home(level, group_ids, sent, grad)
 
 
-def unfold_kernel(flow, *rest):
-    out = rest[-1]
-    rows = flow.shape[1]
-
-    for k in range(out.shape[1]):
-        out[0, k] = flow[0, :, k * rows : (k + 1) * rows]
-
-
-def unfold(level, levels, kinds, flow, base=None):
-    blocks, rows, _ = flow.shape
+def unfold_kernel(level, count, owners, *refs):
+    shares, (out, folded, sems) = refs[:count], refs[-3:]
+    width, rows, _ = shares[0].shape
+    copies = []
+    for s, share in enumerate(shares):
+        for k in range(folded.shape[2]):
+            folded[s, :, k] = share[:, :, k * rows : (k + 1) * rows]
+        to = out.at[level, pl.ds(owners[s] * width, width)]
+        copies.append(pltpu.make_async_copy(folded.at[s], to, sems.at[s]))
+        copies[-1].start()
+    for c in copies:
+        c.wait()
+
+
+def unfold(level, levels, kinds, summed, base=None):
+    shares, owners = summed
+    count = len(shares)
+    width, rows, _ = shares[0].shape
     given = [] if base is None else [base]
     return pl.pallas_call(
-        unfold_kernel,
-        grid=(blocks,),
-        out_shape=jax.ShapeDtypeStruct((levels, blocks, kinds, rows, rows), F32),
-        in_specs=[pl.BlockSpec((1, rows, kinds * rows), lambda b: (b, 0, 0))] + [ANY] * len(given),
-        out_specs=pl.BlockSpec((None, 1, kinds, rows, rows), lambda b: (level, b, 0, 0, 0)),
-        input_output_aliases={1: 0} if given else {},
+        functools.partial(unfold_kernel, level, count),
+        out_shape=jax.ShapeDtypeStruct((levels, width * count, kinds, rows, rows), F32),
+        in_specs=[SMEM] + [VMEM] * count + [ANY] * len(given),
+        out_specs=ANY,
+        scratch_shapes=[
+            pltpu.VMEM((count, width, kinds, rows, rows), F32),
+            pltpu.SemaphoreType.DMA((count,)),
+        ],
+        input_output_aliases={count + 1: 0} if given else {},
         compiler_params=params(),
         cost_estimate=cost(0, 6 * 2**20),
         name="unfold",
-    )(flow, *given)
+    )(owners, *shares, *given)
 
 
 def swap(x):
     return lax.all_to_all(x, "region", split_axis=0, concat_axis=0, tiled=True)
+
+
+def target(i, step, size):
+    return i ^ step if size & (size - 1) == 0 else (i + step) % size
+
+
+def source(i, step, size):
+    return i ^ step if size & (size - 1) == 0 else (i - step) % size
+
+
+def hand(x, step, size):
+    return lax.ppermute(x, "dp", [(i, target(i, step, size)) for i in range(size)])
+
+
+def dp_sum(flow):
+    size, me = lax.axis_size("dp"), lax.axis_index("dp")
+    width = flow.shape[0] // size
+
+    def part(owner):
+        return lax.dynamic_slice_in_dim(flow, owner * width, width, 0)
+
+    parts = [hand(part(target(me, s, size)), s, size) for s in range(1, size)]
+    share = part(me)
+    for p in parts:
+        share = share + p
+    owners = jnp.stack([me] + [source(me, s, size) for s in range(1, size)])
+    return [share] + [hand(share, s, size) for s in range(1, size)], owners
 
 
 def per_device(leaves, weights, groups, prod_kids, sum_kids, cotangent):
@@ -258,6 +305,8 @@
     macs = blocks * rows * rows * kinds * columns
     expos = blocks * kinds * rows * columns
     mib = 2**20
+
+    weight_scratch = [pltpu.VMEM(weights.shape[1:], F32), pltpu.SemaphoreType.DMA]
 
     def call(kernel, outs, scratch, amount, *args, specs, name, out_specs=None):
         return pl.pallas_call(
@@ -273,28 +322,28 @@
 
     outgoing = call(
         functools.partial(pick_kernel, 0), taken_like, [pltpu.SemaphoreType.DMA((slots,))],
-        cost(0, 2 * mib), group_ids, leaves, specs=[SMEM, ANY], out_specs=ANY, name="pick",
+        cost(0, 2 * mib), group_ids, leaves, specs=[SMEM, ANY], name="pick",
     )
     kept = []
     for level in range(levels - 1):
         taken = swap(outgoing)
         outgoing, totals = call(
             functools.partial(forward_kernel, level), (taken_like, level_like),
-            prod_scratch + [pltpu.VMEM((blocks, rows, columns), F32)],
-            cost(24 * macs, 8 * mib, expos), group_ids, kids, lists, taken, weights[level],
-            specs=[SMEM] * 3 + [VMEM] * 2, name="forward",
+            prod_scratch + [pltpu.VMEM((blocks, rows, columns), F32)] + weight_scratch,
+            cost(24 * macs, 8 * mib, expos), group_ids, kids, lists, taken, weights,
+            specs=[SMEM] * 3 + [VMEM, ANY], name="forward",
         )
         kept.append((taken, totals))
     level = levels - 1
     taken = swap(outgoing)
     top, slot_grad, flow = call(
         functools.partial(top_kernel, level, scale), (level_like, taken_like, flow_like),
-        prod_scratch + [prod_grad], cost(72 * macs, 12 * mib, expos),
-        kids, lists, taken, weights[level], cotangent,
-        specs=[SMEM] * 2 + [VMEM] * 3, name="top",
+        prod_scratch + [prod_grad] + weight_scratch, cost(72 * macs, 12 * mib, expos),
+        kids, lists, taken, weights, cotangent,
+        specs=[SMEM] * 2 + [VMEM, ANY, VMEM], name="top",
     )
     sent = swap(slot_grad)
-    flow = lax.psum(flow, "dp")
+    flow = dp_sum(flow)
     weight_flow = unfold(level, levels, kinds, flow)
     for level in reversed(range(levels - 1)):
         taken, totals = kept[level]
@@ -304,14 +353,13 @@
             cost(24 * macs, 8 * mib, expos), group_ids, kids, lists, taken, totals, sent,
             specs=[SMEM] * 3 + [VMEM] * 3, name="flow",
         )
-        part, flow = lax.optimization_barrier((part, flow))
         slot_grad = call(
-            functools.partial(slots_kernel, level), taken_like, prod_scratch + [prod_grad],
-            cost(24 * macs, 8 * mib, expos), kids, lists, taken, weights[level], ratio,
-            specs=[SMEM] * 2 + [VMEM] * 3, name="slots",
+            functools.partial(slots_kernel, level), taken_like, prod_scratch + [prod_grad] + weight_scratch,
+            cost(24 * macs, 8 * mib, expos), kids, lists, taken, weights, ratio,
+            specs=[SMEM] * 2 + [VMEM, ANY, VMEM], name="slots",
         )
         sent = swap(slot_grad)
-        flow = lax.psum(part, "dp")
+        flow = dp_sum(part)
         weight_flow = unfold(level, levels, kinds, flow, weight_flow)
     leaf_grad = call(
         functools.partial(home_kernel, 0), level_like, [], cost(0, 2 * mib), group_ids, sent,

time: 299 us -> 230 us (0.77)
  Pallas kernels: 97.4 us -> 54.7 us
  waiting for transfers between devices: 127 us -> 99.2 us
  starting transfers between devices: 14.6 us -> 28.8 us
  between operations: 14.1 us -> 0.85 us
  other arithmetic: 0 us -> 3.5 us
    psum x2 -> x0, waiting for transfers between devices: 67.8 us -> none  [the longest x1 39.7 us: per_device(): flow = lax.psum(flow, 'dp')]
    ppermute x0 -> x12, waiting for transfers between devices: none -> 52.3 us  [hand(): lax.ppermute(x, 'dp', [(i, target(i, step, size)) for i in range(size)])]
    pallas_call x6, Pallas kernels: 76.8 us -> 47.2 us  [call(): pl.pallas_call(kernel, out_shape=outs, in_specs=specs, out_specs=out_spec...]
    ppermute x0 -> x12, starting transfers between devices: none -> 15.1 us  [hand(): lax.ppermute(x, 'dp', [(i, target(i, step, size)) for i in range(size)])]
    pallas_call x2, Pallas kernels: 20.6 us -> 7.53 us  [unfold(): pl.pallas_call(functools.partial(unfold_kernel, level, count), out_shape=...]
    all_to_all x3, waiting for transfers between devices: 58.5 us -> 46.9 us  [swap(): return lax.all_to_all(x, 'region', split_axis=0, concat_axis=0, tiled=True)]
    squeeze x1 -> x0, local copies, waits for them, and re-layouts: 8.46 us -> none  [per_device(): weights[level]]
    unnamed x13 -> x31, local copies, waits for them, and re-layouts: 3.89 us -> 7.02 us
  transfers between devices with their start and end apart: 5 -> 15, of which waited for: 5 -> 7; matrix products, arithmetic and copies ran while one was open for 3% -> 3% of each run, Pallas kernels for 10% -> 11%
where the time goes in v2:
time: 230 us
  waiting for transfers between devices  99.2 us (43%)
  Pallas kernels  54.7 us (24%)
  blocking collectives  30.8 us (13%)
  starting transfers between devices  28.8 us (13%)
  local copies, waits for them, and re-layouts  11.7 us (5%)
  other arithmetic  3.5 us (2%)
    ppermute x12, waiting for transfers between devices, hand(): lax.ppermute(x, 'dp', [(i, target(i, step, size)) for i in range(size)])  52.3 us
    pallas_call x6, Pallas kernels, call(): pl.pallas_call(kernel, out_shape=outs, in_specs=specs, out_specs=out_spec...  47.2 us
    all_to_all x3, waiting for transfers between devices, swap(): return lax.all_to_all(x, 'region', split_axis=0, concat_axis=0, tiled=True)  46.9 us
    all_to_all x1, blocking collectives, swap(): return lax.all_to_all(x, 'region', split_axis=0, concat_axis=0, tiled=True)  30.8 us
    ppermute x12, starting transfers between devices, hand(): lax.ppermute(x, 'dp', [(i, target(i, step, size)) for i in range(size)])  15.1 us
    all_to_all x3, starting transfers between devices, swap(): return lax.all_to_all(x, 'region', split_axis=0, concat_axis=0, tiled=True)  13.6 us
    pallas_call x2, Pallas kernels, unfold(): pl.pallas_call(functools.partial(unfold_kernel, level, count), out_shape=...  7.53 us
    unnamed x31, local copies, waits for them, and re-layouts  7.02 us
  transfers between devices with their start and end apart: 15, of which 7 were waited for; matrix products, arithmetic and copies ran while one was open for 3% of the time, Pallas kernels for 11%

profile of v2, /device:TPU:0, one launch (start us, length us, event | category | flops | bytes accessed | tf_op | source)
XLA Modules:
  0.0 229.5 jit_solution(6278198710324838464)
XLA Ops:
  0.6 0.8 copy.14
  1.4 0.7 reshape.17.group_ids
  2.1 3.1 %pick.1 = f32[16,64,256]{2,1,0:T(8,128)} custom-call(s32[32]{0:T(128)} %reshape.17.group_ids, f32[16,64,256]{2,1,0:T(8,128)} %source.1), custom_call_target="tpu_custom_call" | custom-call | bytes 2097152 | tf_op jit(solution)/shard_map/pick/pallas_call | solution.py:312
  5.2 6.3 %all-to-all-start = ((f32[16,64,256]{2,1,0:T(8,128)}), f32[16,64,256]{2,1,0:T(8,128)S(1)}, u32[]{:S(2)}, u32[]{:S(2)}) async-start(f32[16,64,256]{2,1,0:T(8,128)} %pick.1), calls=%async_computation | async-start | bytes 2097152 | tf_op jit(solution)/shard_map/all_to_all | solution.py:257
  11.5 0.0 copy-done.12
  11.6 0.1 copy.13
  11.6 0.6 reshape.16.lists
  12.3 0.0 copy-done.13
  12.3 0.1 copy.12
  12.3 0.7 reshape.15.kids
  13.1 25.1 %all-to-all-done.taken = f32[16,64,256]{2,1,0:T(8,128)S(1)} async-done(((f32[16,64,256]{2,1,0:T(8,128)}), f32[16,64,256]{2,1,0:T(8,128)S(1)}, u32[]{:S(2)}, u32[]{:S(2)}) %all-to-all-start) | async-done | bytes 1048608 | tf_op jit(solution)/shard_map/all_to_all | solution.py:257
  38.1 1.0 copy-done.4
  39.1 8.3 %forward.1 = (f32[16,64,256]{2,1,0:T(8,128)}, f32[16,64,256]{2,1,0:T(8,128)}) custom-call(s32[32]{0:T(128)} %reshape.17.group_ids, s32[128]{0:T(128)} %reshape.15.kids, s32[256]{0:T(256)} %reshape.16.lists, f32[16,64,256]{2,1,0:T(8,128)} %copy-done.4, f32[2,16,8,64,64]{4,3,2,1,0:T(8,128)} %all_weights.5), custom_call_target="tpu_custom_call" | custom-call | flops 3221225472 | bytes 8388608 | tf_op jit(solution)/shard_map/forward/pallas_call | solution.py:312
  47.5 30.8 %all_to_all.20.taken = f32[16,64,256]{2,1,0:T(8,128)} all-to-all(f32[16,64,256]{2,1,0:T(8,128)} %get-tuple-element.10), channel_id=1, replica_groups=mesh['dp'=4,'region'=8] {'region'}, dimensions={0} | all-to-all | bytes 2097152 | tf_op jit(solution)/shard_map/all_to_all | solution.py:257
  78.3 14.9 %top.1 = (f32[16,64,256]{2,1,0:T(8,128)}, f32[16,64,256]{2,1,0:T(8,128)}, f32[16,64,512]{2,1,0:T(8,128)}) custom-call(s32[128]{0:T(128)} %reshape.15.kids, s32[256]{0:T(256)} %reshape.16.lists, f32[16,64,256]{2,1,0:T(8,128)} %all_to_all.20.taken, f32[2,16,8,64,64]{4,3,2,1,0:T(8,128)} %all_weights.5, f32[16,64,256]{2,1,0:T(8,128)} %cotangent.1), custom_call_target="tpu_custom_call" | custom-call | flops 9663676416 | bytes 12582912 | tf_op jit(solution)/shard_map/top/pallas_call | solution.py:312
  93.2 0.0 copy-start.1
  93.2 3.7 %all-to-all-start.2 = ((f32[16,64,256]{2,1,0:T(8,128)}), f32[16,64,256]{2,1,0:T(8,128)S(1)}, u32[]{:S(2)}, u32[]{:S(2)}) async-start(f32[16,64,256]{2,1,0:T(8,128)} %get-tuple-element.13), calls=%async_computation.2 | async-start | bytes 2097152 | tf_op jit(solution)/shard_map/all_to_all | solution.py:257
  96.9 0.0 copy-done.1
  96.9 1.2 constant_dynamic-slice_fusion.2
  98.1 1.5 collective-permute-start.6
  99.6 1.5 collective-permute-start.8
  101.1 0.5 collective-permute-start.7
  101.6 21.8 %all-to-all-done.2.sent = f32[16,64,256]{2,1,0:T(8,128)S(1)} async-done(((f32[16,64,256]{2,1,0:T(8,128)}), f32[16,64,256]{2,1,0:T(8,128)S(1)}, u32[]{:S(2)}, u32[]{:S(2)}) %all-to-all-start.2) | async-done | bytes 1048608 | tf_op jit(solution)/shard_map/all_to_all | solution.py:257
  123.4 1.0 copy-done.5
  124.4 7.9 %flow.1 = (f32[16,64,256]{2,1,0:T(8,128)}, f32[16,64,512]{2,1,0:T(8,128)}) custom-call(s32[32]{0:T(128)} %reshape.17.group_ids, s32[128]{0:T(128)} %reshape.15.kids, s32[256]{0:T(256)} %reshape.16.lists, f32[16,64,256]{2,1,0:T(8,128)} %copy-done.4, f32[16,64,256]{2,1,0:T(8,128)} %get-tuple-element.12.totals, f32[16,64,256]{2,1,0:T(8,128)} %copy-done.5), custom_call_target="tpu_custom_call" | custom-call | flops 3221225472 | bytes 8388608 | tf_op jit(solution)/shard_map/flow/pallas_call | solution.py:312
  132.3 10.5 %slots.1 = f32[16,64,256]{2,1,0:T(8,128)} custom-call(s32[128]{0:T(128)} %reshape.15.kids, s32[256]{0:T(256)} %reshape.16.lists, f32[16,64,256]{2,1,0:T(8,128)} %copy-done.4, f32[2,16,8,64,64]{4,3,2,1,0:T(8,128)} %all_weights.5, f32[16,64,256]{2,1,0:T(8,128)} %get-tuple-element.14.ratio), custom_call_target="tpu_custom_call" | custom-call | flops 3221225472 | bytes 8388608 | tf_op jit(solution)/shard_map/slots/pallas_call | solution.py:312
  142.8 3.6 %all-to-all-start.3 = ((f32[16,64,256]{2,1,0:T(8,128)}), f32[16,64,256]{2,1,0:T(8,128)S(1)}, u32[]{:S(2)}, u32[]{:S(2)}) async-start(f32[16,64,256]{2,1,0:T(8,128)} %slots.1), calls=%async_computation.3 | async-start | bytes 2097152 | tf_op jit(solution)/shard_map/all_to_all | solution.py:257
  146.4 1.5 constant_dynamic-slice_fusion.5
  147.8 1.6 collective-permute-start
  149.4 1.5 collective-permute-start.2
  150.9 0.0 collective-permute-done.6
  150.9 0.5 collective-permute-start.1
  151.4 0.0 collective-permute-done.8
  151.4 0.0 collective-permute-done.7
  151.4 1.6 add_add_fusion.refs_0_
  153.0 0.0 copy-start.3
  153.0 2.5 %collective-permute-start.11 = (f32[4,64,512]{2,1,0:T(8,128)S(1)}, f32[4,64,512]{2,1,0:T(8,128)S(1)}, u32[]{:S(2)}, u32[]{:S(2)}) collective-permute-start(f32[4,64,512]{2,1,0:T(8,128)S(1)} %add_add_fusion.refs_0_), channel_id=1, source_target_pairs={{0,24},{8,16},{16,8},{24,0},{1,25},{9,17},{17,9},{25,1},{2,26},{10... | collective-permute-start | bytes 1572872 | tf_op jit(solution)/shard_map/ppermute | solution.py:269
  155.5 0.5 collective-permute-start.10
  156.1 6.6 %collective-permute-done = f32[4,64,512]{2,1,0:T(8,128)S(1)} collective-permute-done((f32[4,64,512]{2,1,0:T(8,128)S(1)}, f32[4,64,512]{2,1,0:T(8,128)S(1)}, u32[]{:S(2)}, u32[]{:S(2)}) %collective-permute-start) | collective-permute-done | bytes 524320 | tf_op jit(solution)/shard_map/ppermute | solution.py:269
  162.7 1.5 collective-permute-start.9
  164.2 10.8 %collective-permute-done.2 = f32[4,64,512]{2,1,0:T(8,128)S(1)} collective-permute-done((f32[4,64,512]{2,1,0:T(8,128)S(1)}, f32[4,64,512]{2,1,0:T(8,128)S(1)}, u32[]{:S(2)}, u32[]{:S(2)}) %collective-permute-start.2) | collective-permute-done | bytes 524320 | tf_op jit(solution)/shard_map/ppermute | solution.py:269
  175.0 13.2 %collective-permute-done.1 = f32[4,64,512]{2,1,0:T(8,128)S(1)} collective-permute-done((f32[4,64,512]{2,1,0:T(8,128)S(1)}, f32[4,64,512]{2,1,0:T(8,128)S(1)}, u32[]{:S(2)}, u32[]{:S(2)}) %collective-permute-start.1) | collective-permute-done | bytes 524320 | tf_op jit(solution)/shard_map/ppermute | solution.py:269
  188.2 1.3 add_add_fusion.1.refs_0_
  189.5 0.0 copy-start.2
  189.5 1.5 collective-permute-start.5
  191.0 1.5 collective-permute-start.4
  192.5 0.0 collective-permute-done.11.refs_3_
  192.5 0.5 collective-permute-start.3
  193.1 0.7 pad_add_fusion.owners
  193.7 17.0 %collective-permute-done.10.refs_2_ = f32[4,64,512]{2,1,0:T(8,128)S(1)} collective-permute-done((f32[4,64,512]{2,1,0:T(8,128)S(1)}, f32[4,64,512]{2,1,0:T(8,128)S(1)}, u32[]{:S(2)}, u32[]{:S(2)}) %collective-permute-start.10) | collective-permute-done | bytes 524320 | tf_op jit(solution)/shard_map/ppermute | solution.py:269
  210.7 0.0 collective-permute-done.9.refs_1_
  210.7 0.8 copy-done.10
  211.5 0.8 copy-done.11
  212.3 3.8 %unfold.2.refs_4_ = f32[2,16,8,64,64]{4,3,2,1,0:T(8,128)} custom-call(s32[4]{0:T(128)} %pad_add_fusion.owners, f32[4,64,512]{2,1,0:T(8,128)} %copy-done.3, f32[4,64,512]{2,1,0:T(8,128)} %copy-done.11, f32[4,64,512]{2,1,0:T(8,128)} %copy-done.10, f32[4,64,512]{2,1,0:T(8,128)} %copy-done.9), custom_call_target="tpu_custom_call" | custom-call | bytes 6291456 | tf_op jit(solution)/shard_map/unfold/pallas_call | solution.py:240
  216.1 0.0 collective-permute-done.5.refs_3_
  216.1 4.7 %collective-permute-done.4.refs_2_ = f32[4,64,512]{2,1,0:T(8,128)S(1)} collective-permute-done((f32[4,64,512]{2,1,0:T(8,128)S(1)}, f32[4,64,512]{2,1,0:T(8,128)S(1)}, u32[]{:S(2)}, u32[]{:S(2)}) %collective-permute-start.4) | collective-permute-done | bytes 524320 | tf_op jit(solution)/shard_map/ppermute | solution.py:269
  220.7 0.0 collective-permute-done.3.refs_1_
  220.7 0.0 copy-done.6
  220.7 0.8 copy-done.7
  221.5 0.8 copy-done.8
  222.3 3.8 %unfold.3 = f32[2,16,8,64,64]{4,3,2,1,0:T(8,128)} custom-call(s32[4]{0:T(128)} %pad_add_fusion.owners, f32[4,64,512]{2,1,0:T(8,128)} %copy-done.2, f32[4,64,512]{2,1,0:T(8,128)} %copy-done.8, f32[4,64,512]{2,1,0:T(8,128)} %copy-done.7, f32[4,64,512]{2,1,0:T(8,128)} %copy-done.6, f32[2,16,8,64,64]{4,3,2,1,0:T(8,128)} %unfold.2.refs_4_), custom_call_target="tpu_custom_call", output_to_operand_aliasing={{}: (5, {})} | custom-call | bytes 6291456 | tf_op jit(solution)/shard_map/unfold/pallas_call | solution.py:240
  226.1 0.0 all-to-all-done.3.sent
  226.1 1.0 copy-done
  227.1 2.4 %home.1 = f32[16,64,256]{2,1,0:T(8,128)} custom-call(s32[32]{0:T(128)} %reshape.17.group_ids, f32[16,64,256]{2,1,0:T(8,128)} %copy-done), custom_call_target="tpu_custom_call" | custom-call | bytes 2097152 | tf_op jit(solution)/shard_map/home/pallas_call | solution.py:312
  (14 shorter events, 0.0 us)
Async XLA Ops:
  2.1 9.5 %copy-start.12 = (s32[2,16,8]{1,2,0:T(8,128)S(1)}, s32[2,16,8]{1,2,0:T(8,128)}, u32[]{:S(2)}) copy-start(s32[2,16,8]{1,2,0:T(8,128)} %param.10) | copy-start | bytes 3076
  2.1 10.2 %copy-start.13 = (s32[2,32,2]{1,2,0:T(2,128)S(1)}, s32[2,32,2]{1,2,0:T(2,128)}, u32[]{:S(2)}) copy-start(s32[2,32,2]{1,2,0:T(2,128)} %param.9) | copy-start | bytes 1540
  5.2 32.9 %all-to-all-start = ((f32[16,64,256]{2,1,0:T(8,128)}), f32[16,64,256]{2,1,0:T(8,128)S(1)}, u32[]{:S(2)}, u32[]{:S(2)}) async-start(f32[16,64,256]{2,1,0:T(8,128)} %pick.1), calls=%async_computation | async-start | bytes 2097152 | tf_op jit(solution)/shard_map/all_to_all | solution.py:257
  38.1 1.0 copy-start.4
  93.2 3.7 %copy-start.1 = (f32[16,64,512]{2,1,0:T(8,128)S(1)}, f32[16,64,512]{2,1,0:T(8,128)}, u32[]{:S(2)}) copy-start(f32[16,64,512]{2,1,0:T(8,128)} %get-tuple-element.16) | copy-start | bytes 6291460
  93.2 30.2 %all-to-all-start.2 = ((f32[16,64,256]{2,1,0:T(8,128)}), f32[16,64,256]{2,1,0:T(8,128)S(1)}, u32[]{:S(2)}, u32[]{:S(2)}) async-start(f32[16,64,256]{2,1,0:T(8,128)} %get-tuple-element.13), calls=%async_computation.2 | async-start | bytes 2097152 | tf_op jit(solution)/shard_map/all_to_all | solution.py:257
  98.1 52.8 %collective-permute-start.6 = (f32[4,64,512]{2,1,0:T(8,128)}, f32[4,64,512]{2,1,0:T(8,128)}, u32[]{:S(2)}, u32[]{:S(2)}) collective-permute-start(f32[4,64,512]{2,1,0:T(8,128)} %get-tuple-element.17), channel_id=1, source_target_pairs={{0,8},{8,0},{16,24},{24,16},{1,9},{9,1},{17,25},{25,17},{2,10},{10... | collective-permute-start | bytes 1572872 | tf_op jit(solution)/shard_map/ppermute | solution.py:269
  99.6 51.8 %collective-permute-start.8 = (f32[4,64,512]{2,1,0:T(8,128)}, f32[4,64,512]{2,1,0:T(8,128)}, u32[]{:S(2)}, u32[]{:S(2)}) collective-permute-start(f32[4,64,512]{2,1,0:T(8,128)} %get-tuple-element.18), channel_id=1, source_target_pairs={{0,24},{8,16},{16,8},{24,0},{1,25},{9,17},{17,9},{25,1},{2,26},{10... | collective-permute-start | bytes 1572872 | tf_op jit(solution)/shard_map/ppermute | solution.py:269
  101.1 50.3 %collective-permute-start.7 = (f32[4,64,512]{2,1,0:T(8,128)}, f32[4,64,512]{2,1,0:T(8,128)}, u32[]{:S(2)}, u32[]{:S(2)}) collective-permute-start(f32[4,64,512]{2,1,0:T(8,128)} %get-tuple-element.19), channel_id=1, source_target_pairs={{0,16},{8,24},{16,0},{24,8},{1,17},{9,25},{17,1},{25,9},{2,18},{10... | collective-permute-start | bytes 1572872 | tf_op jit(solution)/shard_map/ppermute | solution.py:269
  123.4 1.0 copy-start.5
  142.8 83.3 %all-to-all-start.3 = ((f32[16,64,256]{2,1,0:T(8,128)}), f32[16,64,256]{2,1,0:T(8,128)S(1)}, u32[]{:S(2)}, u32[]{:S(2)}) async-start(f32[16,64,256]{2,1,0:T(8,128)} %slots.1), calls=%async_computation.3 | async-start | bytes 2097152 | tf_op jit(solution)/shard_map/all_to_all | solution.py:257
  147.8 14.8 %collective-permute-start = (f32[4,64,512]{2,1,0:T(8,128)S(1)}, f32[4,64,512]{2,1,0:T(8,128)S(1)}, u32[]{:S(2)}, u32[]{:S(2)}) collective-permute-start(f32[4,64,512]{2,1,0:T(8,128)S(1)} %get-tuple-element.20), channel_id=1, source_target_pairs={{0,8},{8,0},{16,24},{24,16},{1,9},{9,1},{17,25},{25,17},{2,10},{10... | collective-permute-start | bytes 1572872 | tf_op jit(solution)/shard_map/ppermute | solution.py:269
  149.4 25.5 %collective-permute-start.2 = (f32[4,64,512]{2,1,0:T(8,128)S(1)}, f32[4,64,512]{2,1,0:T(8,128)S(1)}, u32[]{:S(2)}, u32[]{:S(2)}) collective-permute-start(f32[4,64,512]{2,1,0:T(8,128)S(1)} %get-tuple-element.21), channel_id=1, source_target_pairs={{0,24},{8,16},{16,8},{24,0},{1,25},{9,17},{17,9},{25,1},{2,26},{10... | collective-permute-start | bytes 1572872 | tf_op jit(solution)/shard_map/ppermute | solution.py:269
  150.9 37.3 %collective-permute-start.1 = (f32[4,64,512]{2,1,0:T(8,128)S(1)}, f32[4,64,512]{2,1,0:T(8,128)S(1)}, u32[]{:S(2)}, u32[]{:S(2)}) collective-permute-start(f32[4,64,512]{2,1,0:T(8,128)S(1)} %get-tuple-element.22), channel_id=1, source_target_pairs={{0,16},{8,24},{16,0},{24,8},{1,17},{9,25},{17,1},{25,9},{2,18},{10... | collective-permute-start | bytes 1572872 | tf_op jit(solution)/shard_map/ppermute | solution.py:269
  153.0 57.7 %copy-start.3 = (f32[4,64,512]{2,1,0:T(8,128)}, f32[4,64,512]{2,1,0:T(8,128)S(1)}, u32[]{:S(2)}) copy-start(f32[4,64,512]{2,1,0:T(8,128)S(1)} %add_add_fusion.refs_0_) | copy-start | bytes 1572868
  153.0 39.5 %collective-permute-start.11 = (f32[4,64,512]{2,1,0:T(8,128)S(1)}, f32[4,64,512]{2,1,0:T(8,128)S(1)}, u32[]{:S(2)}, u32[]{:S(2)}) collective-permute-start(f32[4,64,512]{2,1,0:T(8,128)S(1)} %add_add_fusion.refs_0_), channel_id=1, source_target_pairs={{0,24},{8,16},{16,8},{24,0},{1,25},{9,17},{17,9},{25,1},{2,26},{10... | collective-permute-start | bytes 1572872 | tf_op jit(solution)/shard_map/ppermute | solution.py:269
  155.5 55.1 %collective-permute-start.10 = (f32[4,64,512]{2,1,0:T(8,128)S(1)}, f32[4,64,512]{2,1,0:T(8,128)S(1)}, u32[]{:S(2)}, u32[]{:S(2)}) collective-permute-start(f32[4,64,512]{2,1,0:T(8,128)S(1)} %add_add_fusion.refs_0_), channel_id=1, source_target_pairs={{0,16},{8,24},{16,0},{24,8},{1,17},{9,25},{17,1},{25,9},{2,18},{10... | collective-permute-start | bytes 1572872 | tf_op jit(solution)/shard_map/ppermute | solution.py:269
  162.7 48.0 %collective-permute-start.9 = (f32[4,64,512]{2,1,0:T(8,128)S(1)}, f32[4,64,512]{2,1,0:T(8,128)S(1)}, u32[]{:S(2)}, u32[]{:S(2)}) collective-permute-start(f32[4,64,512]{2,1,0:T(8,128)S(1)} %add_add_fusion.refs_0_), channel_id=1, source_target_pairs={{0,8},{8,0},{16,24},{24,16},{1,9},{9,1},{17,25},{25,17},{2,10},{10... | collective-permute-start | bytes 1572872 | tf_op jit(solution)/shard_map/ppermute | solution.py:269
  189.5 26.6 %copy-start.2 = (f32[4,64,512]{2,1,0:T(8,128)}, f32[4,64,512]{2,1,0:T(8,128)S(1)}, u32[]{:S(2)}) copy-start(f32[4,64,512]{2,1,0:T(8,128)S(1)} %add_add_fusion.1.refs_0_) | copy-start | bytes 1572868
  189.5 26.6 %collective-permute-start.5 = (f32[4,64,512]{2,1,0:T(8,128)S(1)}, f32[4,64,512]{2,1,0:T(8,128)S(1)}, u32[]{:S(2)}, u32[]{:S(2)}) collective-permute-start(f32[4,64,512]{2,1,0:T(8,128)S(1)} %add_add_fusion.1.refs_0_), channel_id=1, source_target_pairs={{0,24},{8,16},{16,8},{24,0},{1,25},{9,17},{17,9},{25,1},{2,26},{10... | collective-permute-start | bytes 1572872 | tf_op jit(solution)/shard_map/ppermute | solution.py:269
  191.0 29.7 %collective-permute-start.4 = (f32[4,64,512]{2,1,0:T(8,128)S(1)}, f32[4,64,512]{2,1,0:T(8,128)S(1)}, u32[]{:S(2)}, u32[]{:S(2)}) collective-permute-start(f32[4,64,512]{2,1,0:T(8,128)S(1)} %add_add_fusion.1.refs_0_), channel_id=1, source_target_pairs={{0,16},{8,24},{16,0},{24,8},{1,17},{9,25},{17,1},{25,9},{2,18},{10... | collective-permute-start | bytes 1572872 | tf_op jit(solution)/shard_map/ppermute | solution.py:269
  192.5 18.2 %copy-start.9 = (f32[4,64,512]{2,1,0:T(8,128)}, f32[4,64,512]{2,1,0:T(8,128)S(1)}, u32[]{:S(2)}) copy-start(f32[4,64,512]{2,1,0:T(8,128)S(1)} %collective-permute-done.11.refs_3_) | copy-start | bytes 1572868
  192.5 28.2 %collective-permute-start.3 = (f32[4,64,512]{2,1,0:T(8,128)S(1)}, f32[4,64,512]{2,1,0:T(8,128)S(1)}, u32[]{:S(2)}, u32[]{:S(2)}) collective-permute-start(f32[4,64,512]{2,1,0:T(8,128)S(1)} %add_add_fusion.1.refs_0_), channel_id=1, source_target_pairs={{0,8},{8,0},{16,24},{24,16},{1,9},{9,1},{17,25},{25,17},{2,10},{10... | collective-permute-start | bytes 1572872 | tf_op jit(solution)/shard_map/ppermute | solution.py:269
  210.7 0.8 copy-start.10
  211.5 0.8 copy-start.11
  216.1 4.7 %copy-start.6 = (f32[4,64,512]{2,1,0:T(8,128)}, f32[4,64,512]{2,1,0:T(8,128)S(1)}, u32[]{:S(2)}) copy-start(f32[4,64,512]{2,1,0:T(8,128)S(1)} %collective-permute-done.5.refs_3_) | copy-start | bytes 1572868
  220.7 0.8 copy-start.7
  221.5 0.8 copy-start.8
  226.1 1.0 copy-start
